TPU v7x, 32 devices: a whole 2x2x4 slice. The times are simulated.
32 devices in a mesh: groups: 2 (over x), patch: 16 (over z, y, core).
Axes of the slice: x: 2, y: 2, z: 4, core: 2. Of those that a mesh axis runs over, the one named last changes fastest.
Arguments:
- queries: bfloat16 [4096, 384], P(('groups', 'patch')), parts along dimension 0, may hold values from -112 to 112
- fresh_kv: bfloat16 [2, 4096, 384], P(None, ('groups', 'patch')), parts along dimension 1, may hold values from -4 to 4
- stale_kv: bfloat16 [2, 4096, 384], P(None, 'groups'), parts along dimension 1, may hold values from -4 to 4
- basis_table: float32 [8, 3, 128, 16], replicated, may hold values from -0.5 to 0.5
- token_of_row: int32 [4096], P(('groups', 'patch')), parts along dimension 0, may hold values from 0 to 2047, each once
- step_index: int32 [2], P('groups'), parts along dimension 0, may hold values from 0 to 7
Outputs:
- attended: bfloat16 [4096, 384], P(('groups', 'patch')), parts along dimension 0
There are 2 independent parts, one for each index of `groups`. A program takes and returns all parts, laid end to end along the dimension named above; an argument that names none is the same for every part. Nothing has to cross between parts.
Inputs may be any that keep to these rules, and one draw needn't show every extreme that they name: `token_of_row`: each token appears once.
All inputs are finite; a program needn't handle non-finite values.
Results may differ from a plain program's by a relative error of at most 0.0012.
Values sent between devices are 32-bit elements; how exact they have to be, the bound alone decides.
A program may use at most 192 MiB of HBM per device.

v0:
```python
import functools
import math

import jax
import jax.numpy as jnp
from jax import lax
from jax.experimental import pallas as pl
from jax.experimental.pallas import tpu as pltpu
from jax.sharding import PartitionSpec as P

MESH = pl.DeviceIdType.MESH
TOP = lax.Precision.HIGHEST
F32 = jnp.float32
BF16 = jnp.bfloat16


def dot_nn(a, b, precision=None):
    return lax.dot_general(
        a, b, (((1,), (0,)), ((), ())), precision=precision, preferred_element_type=F32
    )


def dot_nt(a, b, precision=None):
    return lax.dot_general(
        a, b, (((1,), (1,)), ((), ())), precision=precision, preferred_element_type=F32
    )


def split_parts(x, count):
    parts = []
    for _ in range(count):
        part = x.astype(BF16)
        parts.append(part)
        x = x - part.astype(F32)
    return parts


def kernel(
    span,
    tile,
    q_hbm,
    fresh_hbm,
    stale_hbm,
    basis_hbm,
    tok_hbm,
    step_hbm,
    out_ref,
    q_v,
    fresh_v,
    stale_v,
    basis_v,
    tok_v,
    step_s,
    blocks,
    scores,
    spread,
    in_sem,
    send_sem,
    recv_sem,
):
    heads, rank, head_dim = basis_v.shape[1:]
    rows = q_v.shape[0]
    tokens = stale_v.shape[1]
    coef_rows = 2 * heads * rank
    group = lax.axis_index("groups")
    me = lax.axis_index("patch")
    far, near, core = me // 4, (me % 4) // 2, me % 2
    far_peers = [(group, ((far + d) % span) * 4 + near * 2 + core) for d in range(1, span)]
    near_peer = (group, far * 4 + (1 - near) * 2 + core)
    core_peer = (group, far * 4 + near * 2 + (1 - core))

    barrier = pltpu.get_barrier_semaphore()
    for peer in far_peers + [near_peer, core_peer]:
        pl.semaphore_signal(barrier, inc=1, device_id=peer, device_id_type=MESH)

    pairs = [
        (basis_hbm, basis_v),
        (fresh_hbm, fresh_v),
        (tok_hbm, tok_v),
        (q_hbm, q_v),
        (stale_hbm.at[0], stale_v.at[0]),
        (stale_hbm.at[1], stale_v.at[1]),
        (step_hbm, step_s),
    ]
    loads = [pltpu.make_async_copy(s, d, in_sem.at[n]) for n, (s, d) in enumerate(pairs)]
    for load in loads:
        load.start()

    def send(src, dst, peer):
        return pltpu.make_async_remote_copy(
            src_ref=blocks.at[src],
            dst_ref=blocks.at[dst],
            send_sem=send_sem.at[dst],
            recv_sem=recv_sem.at[dst],
            device_id=peer,
            device_id_type=MESH,
        )

    far_sends = [send(0, d, far_peers[d - 1]) for d in range(1, span)]
    near_sends = [send(d, span + d, near_peer) for d in range(span)]
    core_sends = [send(s, 2 * span + s, core_peer) for s in range(2 * span)]

    loads[6].wait()
    loads[0].wait()
    basis = basis_v[step_s[0]]
    basis_t = [basis[h] for h in range(heads)]
    basis_parts = [split_parts(b, 3) for b in basis_t]
    loads[1].wait()
    fresh = fresh_v[...].reshape(2 * rows, heads * head_dim)
    for h in range(heads):
        cols = slice(h * head_dim, (h + 1) * head_dim)
        three = dot_nt(jnp.concatenate(basis_parts[h], axis=0), fresh[:, cols])
        coeffs = three[:rank] + three[rank : 2 * rank] + three[2 * rank :]
        for e in range(2):
            low = (e * heads + h) * rank
            blocks[0, low : low + rank, :] = coeffs[:, e * rows : (e + 1) * rows]
    loads[2].wait()
    blocks[0, coef_rows : coef_rows + 8, :] = jnp.broadcast_to(tok_v[...].astype(F32), (8, rows))

    pl.semaphore_wait(barrier, span + 1)
    for copy in far_sends:
        copy.start()
    near_sends[0].start()
    core_sends[0].start()

    loads[3].wait()
    scale = head_dim ** (-0.5) * math.log2(math.e)
    lane = lax.broadcasted_iota(jnp.int32, (rows, 5 * rank), 1)
    wide_parts, query_parts = [], []
    for h in range(heads):
        head_query = q_v[:, h * head_dim : (h + 1) * head_dim]
        wide = jnp.zeros((rows, 5 * rank), F32)
        for part in reversed(basis_parts[h]):
            wide = wide + dot_nt(head_query, jnp.concatenate([part] * 5, axis=0))
        left = head_query.astype(F32) - dot_nn(wide[:, :rank], basis_t[h], TOP)
        query_parts.append(jnp.concatenate(split_parts(left * scale, 2), axis=0))
        p1, p2, p3 = split_parts(wide * scale, 3)
        picked = jnp.where(
            lane < 2 * rank,
            p1.astype(F32),
            jnp.where(lane < 4 * rank, p2.astype(F32), p3.astype(F32)),
        )
        wide_parts.append(picked.astype(BF16))

    def stale_scores(h):
        cols = slice(h * head_dim, (h + 1) * head_dim)
        for low in range(0, tokens, tile):
            both = dot_nt(query_parts[h], stale_v[0, low : low + tile, cols])
            scores[h, :, low : low + tile] = both[:rows] + both[rows:]

    place_tile = 512

    def place(slots, first):
        lefts, columns = [], []
        for slot in slots:
            parts = split_parts(blocks[slot, :coef_rows, :], 2)
            lefts.append(jnp.concatenate(parts, axis=0))
            tok = blocks[slot, coef_rows : coef_rows + 1, :]
            columns.append(jnp.broadcast_to(tok, (rows, rows)).T)
        left = jnp.concatenate(lefts, axis=1)
        column = jnp.concatenate(columns, axis=0)
        ids = lax.broadcasted_iota(jnp.int32, (column.shape[0], rows), 1).astype(F32)
        shifted = column - ids

        def step(low):
            hots = [
                jnp.where(shifted == float(low + at), 1.0, 0.0).astype(BF16)
                for at in range(0, place_tile, rows)
            ]
            got = dot_nn(left, jnp.concatenate(hots, axis=1))
            if first:
                spread[:, low : low + place_tile] = got
            else:
                spread[:, low : low + place_tile] += got

        for low in range(0, tokens, place_tile):
            step(low)

    def place_all(base, first):
        for at in range(0, span, 4):
            place(range(base + at, base + at + 4), first and at == 0)

    loads[4].wait()
    stale_scores(0)
    for d in range(1, span):
        far_sends[d - 1].wait_recv()
        near_sends[d].start()
        core_sends[d].start()
    for h in range(1, heads):
        stale_scores(h)
    place_all(0, True)
    for d in range(span):
        near_sends[d].wait_recv()
        core_sends[span + d].start()
    for s in range(span):
        core_sends[s].wait_recv()
    place_all(2 * span, False)
    place_all(span, False)
    for s in range(span, 2 * span):
        core_sends[s].wait_recv()
    place_all(3 * span, False)

    loads[5].wait()
    lo_base = coef_rows
    for h in range(heads):
        cols = slice(h * head_dim, (h + 1) * head_dim)
        key_low, value_low = h * rank, (heads + h) * rank
        top = jnp.full((rows, 1), -jnp.inf, F32)
        for low in range(0, tokens, tile):
            span_t = slice(low, low + tile)
            key_hi = spread[key_low : key_low + rank, span_t].astype(BF16)
            key_lo = spread[lo_base + key_low : lo_base + key_low + rank, span_t].astype(BF16)
            right = jnp.concatenate([key_hi, key_lo, key_hi, key_lo, key_hi], axis=0)
            full = scores[h, :, span_t] + dot_nn(wide_parts[h], right)
            scores[h, :, span_t] = full
            top = jnp.maximum(top, jnp.max(full, axis=1, keepdims=True))
        total = jnp.zeros((rows, 1), F32)
        direct = jnp.zeros((2 * rows, head_dim), F32)
        through = jnp.zeros((2 * rows, 2 * rank), F32)
        for low in range(0, tokens, tile):
            span_t = slice(low, low + tile)
            weights = jnp.exp2(scores[h, :, span_t] - top)
            total = total + jnp.sum(weights, axis=1, keepdims=True)
            both = jnp.concatenate(split_parts(weights, 2), axis=0)
            direct = direct + dot_nn(both, stale_v[1, span_t, cols])
            value_hi = spread[value_low : value_low + rank, span_t].astype(BF16)
            value_lo = spread[lo_base + value_low : lo_base + value_low + rank, span_t].astype(BF16)
            through = through + dot_nt(both, jnp.concatenate([value_hi, value_lo], axis=0))
        direct = direct[:rows] + direct[rows:]
        through = through[:rows] + through[rows:]
        own = dot_nt(direct, basis_t[h], TOP)
        twice = jnp.concatenate([basis_t[h], basis_t[h]], axis=0)
        result = direct + dot_nn(through, twice, TOP) - dot_nn(own, basis_t[h], TOP)
        out_ref[:, cols] = (result / total).astype(out_ref.dtype)

    for copy in far_sends + near_sends + core_sends:
        copy.wait_send()


def local(span, queries, fresh_kv, stale_kv, basis_table, token_of_row, step_index):
    steps, heads, head_dim, rank = basis_table.shape
    rows, width = queries.shape
    tokens = stale_kv.shape[1]
    tile = min(tokens, 2048)
    block_rows = 2 * heads * rank + 8
    anywhere = pl.BlockSpec(memory_space=pl.ANY)
    return pl.pallas_call(
        functools.partial(kernel, span, tile),
        out_shape=jax.ShapeDtypeStruct((rows, width), BF16),
        in_specs=[anywhere] * 6,
        out_specs=pl.BlockSpec(memory_space=pltpu.VMEM),
        scratch_shapes=[
            pltpu.VMEM((rows, width), BF16),
            pltpu.VMEM((2, rows, width), BF16),
            pltpu.VMEM((2, tokens, width), BF16),
            pltpu.VMEM((steps, heads, rank, head_dim), F32),
            pltpu.VMEM((1, rows), jnp.int32),
            pltpu.SMEM((1,), jnp.int32),
            pltpu.VMEM((4 * span, block_rows, rows), F32),
            pltpu.VMEM((heads, rows, tokens), F32),
            pltpu.VMEM((4 * heads * rank, tokens), F32),
            pltpu.SemaphoreType.DMA((7,)),
            pltpu.SemaphoreType.DMA((4 * span,)),
            pltpu.SemaphoreType.DMA((4 * span,)),
        ],
        compiler_params=pltpu.CompilerParams(
            collective_id=0, has_side_effects=True, vmem_limit_bytes=60 * 1024 * 1024
        ),
        name="refreshed_attention",
    )(
        queries,
        fresh_kv,
        stale_kv,
        jnp.swapaxes(basis_table, 2, 3),
        token_of_row.reshape(1, rows),
        step_index,
    )


def solution(mesh):
    in_specs = (
        P(("groups", "patch"), None),
        P(None, ("groups", "patch"), None),
        P(None, "groups", None),
        P(),
        P(("groups", "patch")),
        P("groups"),
    )
    out_specs = P(("groups", "patch"), None)
    span = mesh.shape["patch"] // 4
    return jax.shard_map(
        functools.partial(local, span),
        mesh=mesh,
        in_specs=in_specs,
        out_specs=out_specs,
        check_vma=False,
    )
```

profile of v0, /device:TPU:0, one launch (start us, length us, event | category | flops | bytes accessed | tf_op | source)
XLA Modules:
  0.0 23.9 jit_solution(244368213614657844)
XLA Ops:
  0.7 21.7 %refreshed_attention.1 = bf16[128,384]{1,0:T(8,128)(2,1)} custom-call(bf16[128,384]{1,0:T(8,128)(2,1)} %q_hbm.1, bf16[2,128,384]{2,1,0:T(8,128)(2,1)} %fresh_hbm.1, bf16[2,2048,384]{2,1,0:T(8,128)(2,1)} %stale_hbm.1, f32[8,3,16,128]{3,2,1,0:T(8,128)} %bitcast.2, s32[1,128]{1,0:T(1,128)} %bitcast.3, s32[1]{0:T(128)S(6)} %copy.8.step_hbm), custom_call_target="tpu_custom_call" | custom-call | tf_op jit(solution)/shard_map/refreshed_attention/pallas_call | solution.py:247
  22.4 1.5 %copy.9 = bf16[128,384]{1,0:T(8,128)(2,1)} copy(bf16[128,384]{1,0:T(8,128)(2,1)} %refreshed_attention.1) | data formatting | bytes 196608
where the time goes:
time: 24.1 us; the launch traced here: 23.9 us
  Pallas kernels  21.7 us (90%)
  local copies, waits for them, and re-layouts  1.54 us (6%)
  between operations  0.66 us (3%)
    pallas_call x1, Pallas kernels, local(): pl.pallas_call(functools.partial(kernel, span, tile), out_shape=jax.Shape...  21.7 us
    unnamed x1, local copies, waits for them, and re-layouts  1.54 us

commit v1 on v0

--- a/solution.py
+++ b/solution.py
@@ -62,6 +62,7 @@
     rows = q_v.shape[0]
     tokens = stale_v.shape[1]
     coef_rows = 2 * heads * rank
+    lanes = spread.shape[1] // 2
     group = lax.axis_index("groups")
     me = lax.axis_index("patch")
     far, near, core = me // 4, (me % 4) // 2, me % 2
@@ -125,22 +126,26 @@
 
     loads[3].wait()
     scale = head_dim ** (-0.5) * math.log2(math.e)
-    lane = lax.broadcasted_iota(jnp.int32, (rows, 5 * rank), 1)
+    half = heads * rank
+    pad = lanes - 2 * half
+
+    def at_head(part, h):
+        empty = jnp.zeros((rank, head_dim), part.dtype)
+        once = [part if n == h else empty for n in range(heads)]
+        tail = jnp.zeros((pad, head_dim), part.dtype)
+        return jnp.concatenate(once + once + [tail], axis=0)
+
     wide_parts, query_parts = [], []
     for h in range(heads):
         head_query = q_v[:, h * head_dim : (h + 1) * head_dim]
-        wide = jnp.zeros((rows, 5 * rank), F32)
-        for part in reversed(basis_parts[h]):
-            wide = wide + dot_nt(head_query, jnp.concatenate([part] * 5, axis=0))
-        left = head_query.astype(F32) - dot_nn(wide[:, :rank], basis_t[h], TOP)
+        placed = [at_head(part, h) for part in basis_parts[h]]
+        wide = dot_nt(head_query, placed[2])
+        wide = wide + dot_nt(head_query, placed[1])
+        wide = wide + dot_nt(head_query, placed[0])
+        back = dot_nn(wide, at_head(basis_t[h], h), TOP) * 0.5
+        left = head_query.astype(F32) - back
         query_parts.append(jnp.concatenate(split_parts(left * scale, 2), axis=0))
-        p1, p2, p3 = split_parts(wide * scale, 3)
-        picked = jnp.where(
-            lane < 2 * rank,
-            p1.astype(F32),
-            jnp.where(lane < 4 * rank, p2.astype(F32), p3.astype(F32)),
-        )
-        wide_parts.append(picked.astype(BF16))
+        wide_parts.append(jnp.concatenate(split_parts(wide * scale, 2), axis=0))
 
     def stale_scores(h):
         cols = slice(h * head_dim, (h + 1) * head_dim)
@@ -149,32 +154,38 @@
             scores[h, :, low : low + tile] = both[:rows] + both[rows:]
 
     place_tile = 512
+    one_lane = lanes + 2 * half
+    ones = jnp.where(lax.broadcasted_iota(jnp.int32, (1, 2 * lanes), 1) == one_lane, 1.0, 0.0)
 
     def place(slots, first):
-        lefts, columns = [], []
+        rights, row_tokens = [], []
         for slot in slots:
-            parts = split_parts(blocks[slot, :coef_rows, :], 2)
-            lefts.append(jnp.concatenate(parts, axis=0))
-            tok = blocks[slot, coef_rows : coef_rows + 1, :]
-            columns.append(jnp.broadcast_to(tok, (rows, rows)).T)
-        left = jnp.concatenate(lefts, axis=1)
-        column = jnp.concatenate(columns, axis=0)
-        ids = lax.broadcasted_iota(jnp.int32, (column.shape[0], rows), 1).astype(F32)
-        shifted = column - ids
+            hi, lo = split_parts(blocks[slot, :coef_rows, :], 2)
+            empty = jnp.zeros((pad, rows), BF16)
+            rights.append(
+                jnp.concatenate([hi[:half], lo[:half], empty, hi[half:], lo[half:], empty], axis=0)
+            )
+            row_tokens.append(blocks[slot, coef_rows : coef_rows + 1, :])
+        right = jnp.concatenate(rights, axis=1)
 
         def step(low):
-            hots = [
-                jnp.where(shifted == float(low + at), 1.0, 0.0).astype(BF16)
-                for at in range(0, place_tile, rows)
-            ]
-            got = dot_nn(left, jnp.concatenate(hots, axis=1))
+            ids = (lax.broadcasted_iota(jnp.int32, (place_tile, rows), 0) + low).astype(F32)
+            hots = [jnp.where(tok == ids, 1.0, 0.0).astype(BF16) for tok in row_tokens]
+            got = dot_nt(jnp.concatenate(hots, axis=1), right)
+            where = pl.ds(low, place_tile)
             if first:
-                spread[:, low : low + place_tile] = got
+                spread[where, :] = (got + ones).astype(BF16)
             else:
-                spread[:, low : low + place_tile] += got
-
-        for low in range(0, tokens, place_tile):
-            step(low)
+                spread[where, :] += got.astype(BF16)
+
+        if tokens <= 2048:
+            for low in range(0, tokens, place_tile):
+                step(low)
+        else:
+
+            @pl.loop(0, tokens // place_tile)
+            def _(n):
+                step(pl.multiple_of(n * place_tile, place_tile))
 
     def place_all(base, first):
         for at in range(0, span, 4):
@@ -182,55 +193,55 @@
 
     loads[4].wait()
     stale_scores(0)
-    for d in range(1, span):
+    for d in [span - 1] + list(range(1, span - 1)):
         far_sends[d - 1].wait_recv()
         near_sends[d].start()
         core_sends[d].start()
     for h in range(1, heads):
         stale_scores(h)
     place_all(0, True)
+    for s in range(span):
+        core_sends[s].wait_recv()
+    place_all(2 * span, False)
     for d in range(span):
         near_sends[d].wait_recv()
         core_sends[span + d].start()
-    for s in range(span):
-        core_sends[s].wait_recv()
-    place_all(2 * span, False)
+    ends = []
+    for h in range(heads):
+        placed = [at_head(part, h) for part in basis_parts[h]]
+        gram = dot_nn(basis_t[h].T, basis_t[h], TOP)
+        gram_hi, gram_lo = split_parts(-gram, 2)
+        ends.append(
+            jnp.concatenate([gram_hi, placed[0], gram_lo, placed[1], gram_hi, placed[0]], axis=0)
+        )
+
     place_all(span, False)
     for s in range(span, 2 * span):
         core_sends[s].wait_recv()
     place_all(3 * span, False)
 
     loads[5].wait()
-    lo_base = coef_rows
     for h in range(heads):
         cols = slice(h * head_dim, (h + 1) * head_dim)
-        key_low, value_low = h * rank, (heads + h) * rank
         top = jnp.full((rows, 1), -jnp.inf, F32)
         for low in range(0, tokens, tile):
-            span_t = slice(low, low + tile)
-            key_hi = spread[key_low : key_low + rank, span_t].astype(BF16)
-            key_lo = spread[lo_base + key_low : lo_base + key_low + rank, span_t].astype(BF16)
-            right = jnp.concatenate([key_hi, key_lo, key_hi, key_lo, key_hi], axis=0)
-            full = scores[h, :, span_t] + dot_nn(wide_parts[h], right)
-            scores[h, :, span_t] = full
+            part = slice(low, low + tile)
+            both = dot_nt(wide_parts[h], spread[part, :lanes])
+            full = scores[h, :, part] + (both[:rows] + both[rows:])
+            scores[h, :, part] = full
             top = jnp.maximum(top, jnp.max(full, axis=1, keepdims=True))
-        total = jnp.zeros((rows, 1), F32)
-        direct = jnp.zeros((2 * rows, head_dim), F32)
-        through = jnp.zeros((2 * rows, 2 * rank), F32)
+        mixed = jnp.zeros((2 * rows, head_dim + lanes), F32)
         for low in range(0, tokens, tile):
-            span_t = slice(low, low + tile)
-            weights = jnp.exp2(scores[h, :, span_t] - top)
-            total = total + jnp.sum(weights, axis=1, keepdims=True)
+            part = slice(low, low + tile)
+            weights = jnp.exp2(scores[h, :, part] - top)
             both = jnp.concatenate(split_parts(weights, 2), axis=0)
-            direct = direct + dot_nn(both, stale_v[1, span_t, cols])
-            value_hi = spread[value_low : value_low + rank, span_t].astype(BF16)
-            value_lo = spread[lo_base + value_low : lo_base + value_low + rank, span_t].astype(BF16)
-            through = through + dot_nt(both, jnp.concatenate([value_hi, value_lo], axis=0))
-        direct = direct[:rows] + direct[rows:]
-        through = through[:rows] + through[rows:]
-        own = dot_nt(direct, basis_t[h], TOP)
-        twice = jnp.concatenate([basis_t[h], basis_t[h]], axis=0)
-        result = direct + dot_nn(through, twice, TOP) - dot_nn(own, basis_t[h], TOP)
+            right = jnp.concatenate([stale_v[1, part, cols], spread[part, lanes:]], axis=1)
+            mixed = mixed + dot_nn(both, right)
+        mixed = mixed[:rows] + mixed[rows:]
+        total = mixed[:, head_dim + 2 * half : head_dim + 2 * half + 1]
+        mixed_hi, mixed_lo = split_parts(mixed, 2)
+        left = jnp.concatenate([mixed_hi, mixed_hi, mixed_lo], axis=1)
+        result = mixed[:, :head_dim] + dot_nn(left, ends[h])
         out_ref[:, cols] = (result / total).astype(out_ref.dtype)
 
     for copy in far_sends + near_sends + core_sends:
@@ -242,6 +253,7 @@
     rows, width = queries.shape
     tokens = stale_kv.shape[1]
     tile = min(tokens, 2048)
+    lanes = -(-(2 * heads * rank + 1) // 128) * 128
     block_rows = 2 * heads * rank + 8
     anywhere = pl.BlockSpec(memory_space=pl.ANY)
     return pl.pallas_call(
@@ -258,7 +270,7 @@
             pltpu.SMEM((1,), jnp.int32),
             pltpu.VMEM((4 * span, block_rows, rows), F32),
             pltpu.VMEM((heads, rows, tokens), F32),
-            pltpu.VMEM((4 * heads * rank, tokens), F32),
+            pltpu.VMEM((tokens, 2 * lanes), BF16),
             pltpu.SemaphoreType.DMA((7,)),
             pltpu.SemaphoreType.DMA((4 * span,)),
             pltpu.SemaphoreType.DMA((4 * span,)),

time: 24.1 us -> 22.7 us (0.942)
  Pallas kernels: 21.7 us -> 20.4 us
    pallas_call x1, Pallas kernels: 21.7 us -> 20.4 us  [local(): pl.pallas_call(functools.partial(kernel, span, tile), out_shape=jax.Shape...]
where the time goes in v1:
time: 22.7 us; the launch traced here: 22.6 us
  Pallas kernels  20.4 us (90%)
  local copies, waits for them, and re-layouts  1.54 us (7%)
  between operations  0.66 us (3%)
    pallas_call x1, Pallas kernels, local(): pl.pallas_call(functools.partial(kernel, span, tile), out_shape=jax.Shape...  20.4 us
    unnamed x1, local copies, waits for them, and re-layouts  1.54 us

profile of v1, /device:TPU:0, one launch (start us, length us, event | category | flops | bytes accessed | tf_op | source)
XLA Modules:
  0.0 22.6 jit_solution(16892220711988375145)
XLA Ops:
  0.7 20.4 %refreshed_attention.1 = bf16[128,384]{1,0:T(8,128)(2,1)} custom-call(bf16[128,384]{1,0:T(8,128)(2,1)} %q_hbm.1, bf16[2,128,384]{2,1,0:T(8,128)(2,1)} %fresh_hbm.1, bf16[2,2048,384]{2,1,0:T(8,128)(2,1)} %stale_hbm.1, f32[8,3,16,128]{3,2,1,0:T(8,128)} %bitcast.2, s32[1,128]{1,0:T(1,128)} %bitcast.3, s32[1]{0:T(128)S(6)} %copy.8.step_hbm), custom_call_target="tpu_custom_call" | custom-call | tf_op jit(solution)/shard_map/refreshed_attention/pallas_call | solution.py:259
  21.0 1.5 %copy.9 = bf16[128,384]{1,0:T(8,128)(2,1)} copy(bf16[128,384]{1,0:T(8,128)(2,1)} %refreshed_attention.1) | data formatting | bytes 196608
